TPU v7x, 32 devices: a whole 2x2x4 slice. The times are simulated.
32 devices in a mesh: groups: 2 (over x), row: 8 (over z, y), col: 2 (over core).
Axes of the slice: x: 2, y: 2, z: 4, core: 2. Of those that a mesh axis runs over, the one named last changes fastest.
Arguments:
- counts: int32 [2, 8192, 2048], P(None, ('groups', 'row'), 'col'), parts along dimension 1, may hold values from 0 to 255
- row_factors: float32 [8192, 512], P(('groups', 'row', 'col')), parts along dimension 0, may hold values from -1.5 to 1.5
- row_moments: float32 [8192, 512], P(('groups', 'row', 'col')), parts along dimension 0, may hold values from 64 to 32768
- row_bias: float32 [8192], P(('groups', 'row', 'col')), parts along dimension 0, may hold values from -3 to 3
- row_bias_moments: float32 [8192], P(('groups', 'row', 'col')), parts along dimension 0, may hold values from 262144 to 268435456
- col_factors: float32 [32768, 512], P(('groups', 'row', 'col')), parts along dimension 0, may hold values from -1.5 to 1.5
- col_moments: float32 [32768, 512], P(('groups', 'row', 'col')), parts along dimension 0, may hold values from 16 to 8192
- col_bias: float32 [32768], P(('groups', 'row', 'col')), parts along dimension 0, may hold values from -3 to 3
- col_bias_moments: float32 [32768], P(('groups', 'row', 'col')), parts along dimension 0, may hold values from 16384 to 16777216
Outputs:
- row_factors_out: float32 [8192, 512], P(('groups', 'row', 'col')), parts along dimension 0
- row_bias_out: float32 [8192], P(('groups', 'row', 'col')), parts along dimension 0
- col_factors_out: float32 [32768, 512], P(('groups', 'row', 'col')), parts along dimension 0
- col_bias_out: float32 [32768], P(('groups', 'row', 'col')), parts along dimension 0
There are 2 independent parts, one for each index of `groups`. A program takes and returns all parts, laid end to end along the dimension named above; each array names one. Nothing has to cross between parts.
All inputs are finite; a program needn't handle non-finite values.
Results may differ from a plain program's by a relative error of at most 0.0066.
Values may be sent and summed in bfloat16 or wider, within the bound.
A program may use at most 64 MiB of HBM per device.

v0:
```python
import jax
import jax.numpy as jnp
from jax import lax
from jax.sharding import PartitionSpec as P

ROUNDS = 2


LEARN_RATE = 0.25
COUNT_SCALE = 100.0
WEIGHT_POWER = 0.75


def from_behind(value, axis, steps):
    count = lax.axis_size(axis)
    pairs = [(source, (source + steps) % count) for source in range(count)]
    return lax.ppermute(value, axis, pairs)


def weights_logs(counts):
    values = counts.astype(jnp.float32)
    weight = jnp.minimum((values / COUNT_SCALE) ** WEIGHT_POWER, 1.0)
    log_count = jnp.log(jnp.maximum(values, 1.0))
    return (weight, log_count)


def adagrad(current, moment, gradient):
    moment = moment + gradient * gradient
    return (current - LEARN_RATE * gradient / jnp.sqrt(moment), moment)


def tile_grads(counts_now, gathered, offsets, col_block, block_offsets):
    weight, log_count = weights_logs(counts_now)
    col_low = col_block.astype(jnp.bfloat16)
    predicted = lax.dot_general(
        gathered, col_low, (((1,), (1,)), ((), ())), preferred_element_type=jnp.float32
    )
    residue = weight * (predicted + offsets[:, None] + block_offsets[None, :] - log_count)
    residue_low = residue.astype(jnp.bfloat16)
    grad_rows = jnp.dot(residue_low, col_low, preferred_element_type=jnp.float32)
    grad_block = lax.dot_general(
        residue_low, gathered, (((0,), (0,)), ((), ())), preferred_element_type=jnp.float32
    )
    return (grad_rows, jnp.sum(residue, axis=1), grad_block, jnp.sum(residue, axis=0))


def per_device(
    counts,
    row_factors,
    row_moments,
    row_bias,
    row_bias_moments,
    col_factors,
    col_moments,
    col_bias,
    col_bias_moments,
):
    row_value, row_moment, row_level, row_level_mom = (
        row_factors,
        row_moments,
        row_bias,
        row_bias_moments,
    )
    col_value, col_moment, col_level, col_level_mom = (
        col_factors,
        col_moments,
        col_bias,
        col_bias_moments,
    )
    for number in range(ROUNDS):
        counts_now = counts[number]
        gathered = lax.all_gather(row_value.astype(jnp.bfloat16), "col", axis=0, tiled=True)
        offsets = lax.all_gather(row_level, "col", axis=0, tiled=True)
        if number > 0:
            col_value, col_moment, col_level, col_level_mom = from_behind(
                (col_value, col_moment, col_level, col_level_mom), "row", -1
            )
        col_block, block_offsets = (col_value, col_level)
        grad_rows, grad_offsets, grad_block, grad_block_offsets = tile_grads(
            counts_now, gathered, offsets, col_block, block_offsets
        )
        col_value, col_moment = adagrad(col_value, col_moment, grad_block)
        col_level, col_level_mom = adagrad(col_level, col_level_mom, grad_block_offsets)
        grad_rows, grad_offsets = (
            lax.psum_scatter(grad_rows, "col", scatter_dimension=0, tiled=True),
            lax.psum_scatter(grad_offsets, "col", scatter_dimension=0, tiled=True),
        )
        row_value, row_moment = adagrad(row_value, row_moment, grad_rows)
        row_level, row_level_mom = adagrad(row_level, row_level_mom, grad_offsets)
    col_value, col_level = from_behind((col_value, col_level), "row", ROUNDS - 1)
    return (row_value, row_level, col_value, col_level)


def solution(mesh):
    in_specs = (
        P(None, ("groups", "row"), "col"),
        P(("groups", "row", "col"), None),
        P(("groups", "row", "col"), None),
        P(("groups", "row", "col")),
        P(("groups", "row", "col")),
        P(("groups", "row", "col"), None),
        P(("groups", "row", "col"), None),
        P(("groups", "row", "col")),
        P(("groups", "row", "col")),
    )
    out_specs = (
        P(("groups", "row", "col"), None),
        P(("groups", "row", "col")),
        P(("groups", "row", "col"), None),
        P(("groups", "row", "col")),
    )
    return jax.shard_map(
        per_device, mesh=mesh, in_specs=in_specs, out_specs=out_specs, check_vma=False
    )
```

profile of v0, /device:TPU:0, one launch (start us, length us, event | category | flops | bytes accessed | tf_op | source)
XLA Modules:
  0.0 194.4 jit_solution(12473363125663666981)
XLA Ops:
  7.2 0.0 reduce-scatter.3.cloned.1.call-start
  7.2 2.1 %all-gather = f32[2,1,256]{2,1,0:T(1,128)S(1)} all-gather(f32[1,1,256]{2,1,0:T(1,128)} %bitcast.26), channel_id=1, replica_groups=mesh['groups'=2,'row'=8,'col'=2] {'col'}, dimensions={0}, use_global_device_ids=true | all-gather | bytes 3072 | tf_op jit(solution)/shard_map/all_gather | solution.py:73
  9.3 1.1 convert_element_type.27
  10.4 2.2 %all_gather.12 = bf16[512,512]{1,0:T(8,128)(2,1)S(1)} all-gather(bf16[256,512]{1,0:T(8,128)(2,1)S(1)} %convert_element_type.27), channel_id=1, replica_groups=mesh['groups'=2,'row'=8,'col'=2] {'col'}, dimensions={0}, use_global_device_ids=true | all-gather | bytes 786432 | tf_op jit(solution)/shard_map/all_gather | solution.py:72
  12.6 0.0 copy-start.5
  12.6 0.0 copy-start
  12.6 4.8 %fusion.21 = (f32[512]{0:T(512)S(1)}, f32[1024]{0:T(1024)S(1)}, bf16[512,1024]{1,0:T(8,128)(2,1)S(1)}) fusion(f32[1024]{0:T(1024)} %param.16, f32[512]{0:T(512)S(1)} %bitcast.28, bf16[512,512]{1,0:T(8,128)(2,1)S(1)} %all_gather.12, f32[1024,512]{1,0:T(8,128)} %param.14, s32[2,512,1024]{2,1,0:T(8,128)} %param.9), kind=kOutput, calls=%fused_computation.31 | convolution fusion | flops 543160832 | bytes 5779456 | tf_op jit(solution)/shard_map/dot_general | solution.py:35
  17.4 0.0 copy-done.5
  17.4 0.0 copy-start.3
  17.4 1.0 copy-done.3
  18.4 0.0 copy-done
  18.4 1.7 fusion.15
  20.1 0.0 reduce-scatter.3.cloned.1.call-update
  20.1 0.0 copy-start.7
  20.1 0.0 copy-start.8
  20.1 0.0 copy-start.11
  20.1 0.0 copy-start.9
  20.2 0.0 copy-start.10
  20.2 0.0 copy-start.1
  20.2 0.0 copy-start.4
  20.2 0.0 reduce-scatter.5.cloned.1.call-start
  20.2 5.1 %multiply_subtract_fusion.1 = (f32[1024,512]{1,0:T(8,128)}, f32[1024,512]{1,0:T(8,128)}) fusion(f32[1024,512]{1,0:T(8,128)S(1)} %copy-done, f32[1024,512]{1,0:T(8,128)} %param.15, bf16[512,512]{1,0:T(8,128)(2,1)} %copy-done.5, bf16[512,1024]{1,0:T(8,128)(2,1)} %copy-done.3), kind=kOutput, calls=%fused_computation.5 | convolution fusion | flops 539492352 | bytes 9961472 | tf_op jit(solution)/shard_map/dot_general | solution.py:41
  25.3 5.9 %collective-permute-start = (f32[1024,512]{1,0:T(8,128)}, f32[1024,512]{1,0:T(8,128)S(1)}, u32[]{:S(2)}, u32[]{:S(2)}) collective-permute-start(f32[1024,512]{1,0:T(8,128)} %get-tuple-element.8), channel_id=1, source_target_pairs={{0,14},{2,0},{4,2},{6,4},{8,6},{10,8},{12,10},{14,12},{1,15},{3,1}... | collective-permute-start | bytes 6291464 | tf_op jit(solution)/shard_map/ppermute | solution.py:17
  31.2 0.5 collective-permute-start.2
  31.7 0.0 copy-done.7
  31.7 0.0 copy-done.8
  31.7 1.5 collective-permute-start.1
  33.2 0.0 copy-done.11
  33.2 0.6 dynamic-slice
  34.4 2.5 %all-reduce = f32[512]{0:T(512)S(1)} all-reduce(f32[512]{0:T(512)S(1)} %get-tuple-element.6), channel_id=3, replica_groups=mesh['groups'=2,'row'=8,'col'=2] {'col'}, use_global_device_ids=true, to_apply=%region_2.0.clone | all-reduce | flops 512 | bytes 4096
  36.9 0.0 copy-done.9
  36.9 0.0 copy-done.10
  36.9 0.1 multiply_subtract_fusion.7
  37.0 1.8 all-gather.1
  38.8 0.0 reduce-scatter.3.cloned.1.call-done
  38.8 0.0 copy-done.1
  38.8 0.0 copy-done.4
  38.8 1.2 fusion.19
  40.0 2.2 %all_gather.14 = bf16[512,512]{1,0:T(8,128)(2,1)S(1)} all-gather(bf16[256,512]{1,0:T(8,128)(2,1)S(1)} %fusion.19), channel_id=1, replica_groups=mesh['groups'=2,'row'=8,'col'=2] {'col'}, dimensions={0}, use_global_device_ids=true | all-gather | bytes 786432 | tf_op jit(solution)/shard_map/all_gather | solution.py:72
  42.2 0.0 copy-start.6
  42.2 79.6 %collective-permute-done.1 = f32[1024]{0:T(1024)S(1)} collective-permute-done((f32[1024]{0:T(1024)S(1)}, f32[1024]{0:T(1024)S(1)}, u32[]{:S(2)}, u32[]{:S(2)}) %collective-permute-start.1) | collective-permute-done | bytes 4128 | tf_op jit(solution)/shard_map/ppermute | solution.py:17
  121.8 0.0 collective-permute-done
  121.8 3.9 %fusion.20 = (f32[1024]{0:T(1024)S(1)}, f32[512]{0:T(512)S(1)}, bf16[512,1024]{1,0:T(8,128)(2,1)S(1)}) fusion(f32[1024]{0:T(1024)S(1)} %collective-permute-done.1, f32[512]{0:T(512)S(1)} %bitcast.27, bf16[512,512]{1,0:T(8,128)(2,1)S(1)} %all_gather.14, f32[1024,512]{1,0:T(8,128)S(1)} %collective-permute-done, s32[2,512,1024]{2,1,0:T(8,128)} %param.9), kind=kOutput, calls=%fused_computation.30 | convolution fusion | flops 543160832 | bytes 5779456 | tf_op jit(solution)/shard_map/dot_general | solution.py:35
  125.7 0.0 copy-done.6
  125.7 0.0 copy-start.2
  125.7 1.0 copy-done.2
  126.7 1.7 fusion.4
  128.4 0.0 reduce-scatter.5.cloned.1.call-update
  128.4 0.0 collective-permute-done.2
  128.4 4.3 %multiply_subtract_fusion = f32[1024,512]{1,0:T(8,128)} fusion(f32[1024,512]{1,0:T(8,128)S(1)} %collective-permute-done, f32[1024,512]{1,0:T(8,128)} %collective-permute-done.2, bf16[512,512]{1,0:T(8,128)(2,1)} %copy-done.6, bf16[512,1024]{1,0:T(8,128)(2,1)} %copy-done.2), kind=kOutput, calls=%fused_computation.4 | convolution fusion | flops 539492352 | bytes 7864320 | tf_op jit(solution)/shard_map/dot_general | solution.py:41
  132.8 0.3 collective-permute-start.3
  133.1 4.8 %collective-permute-start.4 = (f32[1024]{0:T(1024)S(1)}, f32[1024]{0:T(1024)S(1)}, u32[]{:S(2)}, u32[]{:S(2)}) collective-permute-start(f32[1024]{0:T(1024)S(1)} %get-tuple-element.11), channel_id=1, source_target_pairs={{0,14},{2,0},{4,2},{6,4},{8,6},{10,8},{12,10},{14,12},{1,15},{3,1}... | collective-permute-start | bytes 12296 | tf_op jit(solution)/shard_map/ppermute | solution.py:17
  137.9 1.3 collective-permute-done.4
  139.3 0.0 collective-permute-start.5
  139.3 2.5 %all-reduce.1 = f32[512]{0:T(512)S(1)} all-reduce(f32[512]{0:T(512)S(1)} %get-tuple-element.5), channel_id=5, replica_groups=mesh['groups'=2,'row'=8,'col'=2] {'col'}, use_global_device_ids=true, to_apply=%region_6.0.clone | all-reduce | flops 512 | bytes 4096
  141.8 0.6 multiply_subtract_fusion.6
  142.4 41.0 %collective-permute-done.5 = f32[1024]{0:T(1024)S(1)} collective-permute-done((f32[1024]{0:T(1024)S(1)}, f32[1024]{0:T(1024)S(1)}, u32[]{:S(2)}, u32[]{:S(2)}) %collective-permute-start.5) | collective-permute-done | bytes 4128 | tf_op jit(solution)/shard_map/ppermute | solution.py:17
  183.4 0.0 reduce-scatter.5.cloned.1.call-done
  183.4 2.2 %multiply_subtract_fusion.2 = f32[256,512]{1,0:T(8,128)} fusion(f32[256,512]{1,0:T(8,128)} %reduce-scatter.5.cloned.1.call-done, f32[256,512]{1,0:T(8,128)S(1)} %copy-done.4, f32[256,512]{1,0:T(8,128)} %reduce-scatter.3.cloned.1.call-done, f32[256,512]{1,0:T(8,128)S(1)} %copy-done.1), kind=kLoop, calls=%fused_computation.7 | loop fusion | flops 1310720 | bytes 2621440 | tf_op jit(solution)/shard_map/sub | solution.py:29
  185.7 0.0 collective-permute-done.3
  185.7 1.3 copy.15
  187.0 0.6 copy.16
  (2 shorter events, 0.0 us)
Async XLA Ops:
  7.2 31.6 %reduce-scatter.3.cloned.1.call-start = ((), (), s32[]{:S(2)}) async-start(), calls=%async_computation.2 | async-start | bytes 1572864 | tf_op jit(solution)/shard_map/reduce_scatter | solution.py:85
  12.6 4.8 %copy-start.5 = (bf16[512,512]{1,0:T(8,128)(2,1)}, bf16[512,512]{1,0:T(8,128)(2,1)S(1)}, u32[]{:S(2)}) copy-start(bf16[512,512]{1,0:T(8,128)(2,1)S(1)} %all_gather.12) | copy-start | bytes 1572868
  12.6 5.8 %copy-start = (f32[1024,512]{1,0:T(8,128)S(1)}, f32[1024,512]{1,0:T(8,128)}, u32[]{:S(2)}) copy-start(f32[1024,512]{1,0:T(8,128)} %param.14) | copy-start | bytes 6291460
  17.4 1.0 copy-start.3
  20.1 11.6 %copy-start.7 = (f32[1024]{0:T(1024)S(1)}, f32[1024]{0:T(1024)}, u32[]{:S(2)}) copy-start(f32[1024]{0:T(1024)} %param.16) | copy-start | bytes 12292
  20.1 11.6 %copy-start.8 = (f32[1024]{0:T(1024)S(1)}, f32[1024]{0:T(1024)}, u32[]{:S(2)}) copy-start(f32[1024]{0:T(1024)} %param.17) | copy-start | bytes 12292
  20.1 13.1 %copy-start.11 = (u32[32]{0:T(128)S(1)}, u32[32]{0:T(128)}, u32[]{:S(2)}) copy-start(u32[32]{0:T(128)} %constant.17) | copy-start | bytes 388
  20.1 16.8 %copy-start.9 = (f32[256]{0:T(256)S(1)}, f32[256]{0:T(256)}, u32[]{:S(2)}) copy-start(f32[256]{0:T(256)} %param.12) | copy-start | bytes 3076
  20.2 16.7 %copy-start.10 = (f32[256]{0:T(256)S(1)}, f32[256]{0:T(256)}, u32[]{:S(2)}) copy-start(f32[256]{0:T(256)} %param.13) | copy-start | bytes 3076
  20.2 18.6 %copy-start.1 = (f32[256,512]{1,0:T(8,128)S(1)}, f32[256,512]{1,0:T(8,128)}, u32[]{:S(2)}) copy-start(f32[256,512]{1,0:T(8,128)} %param.10) | copy-start | bytes 1572868
  20.2 18.6 %copy-start.4 = (f32[256,512]{1,0:T(8,128)S(1)}, f32[256,512]{1,0:T(8,128)}, u32[]{:S(2)}) copy-start(f32[256,512]{1,0:T(8,128)} %param.11) | copy-start | bytes 1572868
  20.2 163.2 %reduce-scatter.5.cloned.1.call-start = ((), (), s32[]{:S(2)}) async-start(), calls=%async_computation.3 | async-start | bytes 1572864 | tf_op jit(solution)/shard_map/reduce_scatter | solution.py:85
  25.3 96.4 %collective-permute-start = (f32[1024,512]{1,0:T(8,128)}, f32[1024,512]{1,0:T(8,128)S(1)}, u32[]{:S(2)}, u32[]{:S(2)}) collective-permute-start(f32[1024,512]{1,0:T(8,128)} %get-tuple-element.8), channel_id=1, source_target_pairs={{0,14},{2,0},{4,2},{6,4},{8,6},{10,8},{12,10},{14,12},{1,15},{3,1}... | collective-permute-start | bytes 6291464 | tf_op jit(solution)/shard_map/ppermute | solution.py:17
  31.2 97.2 %collective-permute-start.2 = (f32[1024,512]{1,0:T(8,128)}, f32[1024,512]{1,0:T(8,128)}, u32[]{:S(2)}, u32[]{:S(2)}) collective-permute-start(f32[1024,512]{1,0:T(8,128)} %get-tuple-element.9), channel_id=1, source_target_pairs={{0,14},{2,0},{4,2},{6,4},{8,6},{10,8},{12,10},{14,12},{1,15},{3,1}... | collective-permute-start | bytes 6291464 | tf_op jit(solution)/shard_map/ppermute | solution.py:17
  31.7 90.0 %collective-permute-start.1 = (f32[1024]{0:T(1024)S(1)}, f32[1024]{0:T(1024)S(1)}, u32[]{:S(2)}, u32[]{:S(2)}) collective-permute-start(f32[1024]{0:T(1024)S(1)} %get-tuple-element.10), channel_id=1, source_target_pairs={{0,14},{2,0},{4,2},{6,4},{8,6},{10,8},{12,10},{14,12},{1,15},{3,1}... | collective-permute-start | bytes 12296 | tf_op jit(solution)/shard_map/ppermute | solution.py:17
  42.2 83.5 %copy-start.6 = (bf16[512,512]{1,0:T(8,128)(2,1)}, bf16[512,512]{1,0:T(8,128)(2,1)S(1)}, u32[]{:S(2)}) copy-start(bf16[512,512]{1,0:T(8,128)(2,1)S(1)} %all_gather.14) | copy-start | bytes 1572868
  125.7 1.0 copy-start.2
  132.8 52.9 %collective-permute-start.3 = (f32[1024,512]{1,0:T(8,128)}, f32[1024,512]{1,0:T(8,128)S(1)}, u32[]{:S(2)}, u32[]{:S(2)}) collective-permute-start(f32[1024,512]{1,0:T(8,128)} %multiply_subtract_fusion), channel_id=1, source_target_pairs={{0,2},{2,4},{4,6},{6,8},{8,10},{10,12},{12,14},{14,0},{1,3},{3,5},... | collective-permute-start | bytes 6291464 | tf_op jit(solution)/shard_map/ppermute | solution.py:17
  133.1 6.2 %collective-permute-start.4 = (f32[1024]{0:T(1024)S(1)}, f32[1024]{0:T(1024)S(1)}, u32[]{:S(2)}, u32[]{:S(2)}) collective-permute-start(f32[1024]{0:T(1024)S(1)} %get-tuple-element.11), channel_id=1, source_target_pairs={{0,14},{2,0},{4,2},{6,4},{8,6},{10,8},{12,10},{14,12},{1,15},{3,1}... | collective-permute-start | bytes 12296 | tf_op jit(solution)/shard_map/ppermute | solution.py:17
  139.3 44.2 %collective-permute-start.5 = (f32[1024]{0:T(1024)S(1)}, f32[1024]{0:T(1024)S(1)}, u32[]{:S(2)}, u32[]{:S(2)}) collective-permute-start(f32[1024]{0:T(1024)S(1)} %multiply_subtract_fusion.4), channel_id=1, source_target_pairs={{0,2},{2,4},{4,6},{6,8},{8,10},{10,12},{12,14},{14,0},{1,3},{3,5},... | collective-permute-start | bytes 12296 | tf_op jit(solution)/shard_map/ppermute | solution.py:17
Sparse Core Ops, SparseCore 0:
  20.2 11.0 reduce-scatter.2
  128.5 10.3 reduce-scatter.4
where the time goes:
time: 195 us; the launch traced here: 194 us
  waiting for transfers between devices  122 us (63%)
  matrix products  21.5 us (11%)
  between operations  14.8 us (8%)
  blocking collectives  13.2 us (7%)
  starting transfers between devices  13.1 us (7%)
  other arithmetic  5.27 us (3%)
  local copies, waits for them, and re-layouts  4.54 us (2%)
    ppermute x6, waiting for transfers between devices, from_behind(): return lax.ppermute(value, axis, pairs)  122 us
    ppermute x6, starting transfers between devices, from_behind(): return lax.ppermute(value, axis, pairs)  13 us
    dot_general x2, matrix products, tile_grads(): lax.dot_general(residue_low, gathered, (((0,), (0,)), ((), ())), preferre...  9.43 us
    dot_general x2, matrix products, tile_grads(): lax.dot_general(gathered, col_low, (((1,), (1,)), ((), ())), preferred_el...  8.68 us
    unnamed x2, blocking collectives  4.94 us
    unnamed x27, local copies, waits for them, and re-layouts  4.54 us
    all_gather x2, blocking collectives, per_device(): lax.all_gather(row_value.astype(jnp.bfloat16), 'col', axis=0, tiled=True)  4.36 us
    all_gather x2, blocking collectives, per_device(): offsets = lax.all_gather(row_level, 'col', axis=0, tiled=True)  3.91 us
  transfers between devices with their start and end apart: 8, of which 3 were waited for; matrix products, arithmetic and copies ran while one was open for 10% of the time, Pallas kernels for 0%

commit v1 on v0

v1 whole, which is shorter than its diff:
```python
import functools
import math

import jax
import jax.numpy as jnp
from jax import lax
from jax.experimental import pallas as pl
from jax.experimental.pallas import tpu as pltpu
from jax.sharding import PartitionSpec as P


LEARN_RATE = 0.25
COUNT_SCALE = 100.0
WEIGHT_POWER = 0.75
CHUNKS = 4
EARLY = 2
SUB = 16
LANES = 128
MESH = pl.DeviceIdType.MESH
F32 = jnp.float32
BF16 = jnp.bfloat16


def step(value, moment, grad):
    moment = moment + grad * grad
    return value - LEARN_RATE * grad * lax.rsqrt(moment), moment


def to_column(line):
    return jnp.transpose(jnp.broadcast_to(line, (LANES, line.shape[1])))


def to_line(column):
    return jnp.sum(jnp.transpose(column), axis=0, keepdims=True)


def kernel(
    ring,
    counts, row_factors, row_moments, row_bias, row_bias_mom,
    col_factors, col_moments, col_bias, col_bias_mom,
    row_out, row_bias_out, col_out, col_bias_out,
    c0, c1, vrow, vrmom, vcol, vcmom, col_low,
    rows0, rb0, rows1, rb1, rsend, rbsend, snd, rcv,
    pred, res, rbc, bacc, gro, gin, gob, gib, gc, gcb,
    rbm, cbias, cbm,
    xs, xr, bs, br, xsb, xrb, bsb, brb,
    lsem, osem, ssem, rsem, csem, ksem, xsem, ysem,
    bsem, dsem,
):
    me = lax.axis_index("row")
    mine = lax.axis_index("col")
    other = 1 - mine
    right = lax.rem(me + 1, ring)
    left = lax.rem(me + ring - 1, ring)
    half = vrow.shape[0]
    part = half // CHUNKS
    cols = vcol.shape[0]

    def local(src, dst, k):
        cp = pltpu.make_async_copy(src, dst, lsem.at[k])
        cp.start()
        return cp

    def remote(src, dst, s, r, **where):
        return pltpu.make_async_remote_copy(
            src_ref=src, dst_ref=dst, send_sem=s, recv_sem=r,
            device_id=where, device_id_type=MESH,
        )

    in_row = local(row_factors, vrow, 0)
    in_c1 = [
        local(counts.at[1, :, pl.ds(j * part, part), :], c1.at[j], 1 + j)
        for j in range(CHUNKS)
    ]
    in_col = local(col_factors, vcol, 1 + CHUNKS)
    in_c0 = local(counts.at[0], c0, 2 + CHUNKS)
    in_rmom = local(row_moments, vrmom, 3 + CHUNKS)
    in_cmom = local(col_moments, vcmom, 4 + CHUNKS)

    barrier = pltpu.get_barrier_semaphore()
    pl.semaphore_signal(barrier, inc=1, device_id={"row": left}, device_id_type=MESH)
    pl.semaphore_signal(barrier, inc=1, device_id={"row": right}, device_id_type=MESH)
    pl.semaphore_signal(barrier, inc=1, device_id={"col": other}, device_id_type=MESH)

    in_row.wait()
    rows0[mine] = vrow[...].astype(BF16)
    rb0[mine] = row_bias[...]
    pl.semaphore_wait(barrier, 3)
    swap_rows = remote(rows0.at[mine], rows0.at[mine], ssem.at[0], rsem.at[0], col=other)
    swap_rows.start()
    swap_rb = remote(rb0.at[mine], rb0.at[mine], ssem.at[1], rsem.at[1], col=other)
    swap_rb.start()

    send_counts = [
        remote(snd.at[j], rcv.at[j], csem.at[j], ksem.at[j], row=right)
        for j in range(CHUNKS)
    ]

    def push(j):
        in_c1[j].wait()
        for s in (0, 1):
            snd[j, pl.ds(s * part, part)] = c1[j, s].astype(F32).astype(BF16)
        send_counts[j].start()

    for j in range(EARLY):
        push(j)

    in_col.wait()
    col_low[...] = vcol[...].astype(BF16)
    cbias[...] = col_bias[...]
    cbm[...] = col_bias_mom[...]
    rbm[...] = row_bias_mom[...]
    gc[...] = jnp.zeros_like(gc)
    gcb[...] = jnp.zeros_like(gcb)

    def tile(rows, column_bias, load, store_sum):
        count = rows.shape[0]
        rbc[0:count] = column_bias
        pred[0:count] = lax.dot_general(
            rows, col_low[...], (((1,), (1,)), ((), ())), preferred_element_type=F32
        )

        def body(s, carry):
            o = pl.multiple_of(s * SUB, SUB)
            x = load(o)
            logs = jnp.log(jnp.maximum(x, 1.0))
            weight = jnp.exp(WEIGHT_POWER * (logs - math.log(COUNT_SCALE)))
            weight = jnp.where(x >= 1.0, jnp.minimum(weight, 1.0), 0.0)
            bias = rbc[pl.ds(o, SUB)][:, 0:1]
            value = weight * (pred[pl.ds(o, SUB)] + bias + cbias[...] - logs)
            res[pl.ds(o, SUB)] = value.astype(BF16)
            total = value[:, 0:LANES]
            for k in range(1, cols // LANES):
                total = total + value[:, k * LANES:(k + 1) * LANES]
            rbc[pl.ds(o, SUB)] = total
            down = value[0:8]
            for k in range(1, SUB // 8):
                down = down + value[k * 8:(k + 1) * 8]
            gcb[...] += down
            return carry

        lax.fori_loop(0, count // SUB, body, 0)
        store_sum(rbc[0:count])
        low = res[0:count]
        grad_rows = jnp.dot(low, col_low[...], preferred_element_type=F32)
        gc[...] += lax.dot_general(
            low, rows, (((0,), (0,)), ((), ())), preferred_element_type=F32
        )
        return grad_rows

    def half_tile(which):
        def load(o):
            return c0[which, pl.ds(o, SUB)].astype(F32)

        def store_sum(total):
            gob[which] = to_line(total)

        gro[which] = tile(rows0[which], to_column(rb0[which]), load, store_sum)

    swap_rows.wait()
    swap_rb.wait()
    in_c0.wait()
    half_tile(other)
    swap_gr = remote(gro.at[other], gin, ssem.at[2], rsem.at[2], col=other)
    swap_gr.start()
    swap_gb = remote(gob.at[other], gib, ssem.at[3], rsem.at[3], col=other)
    swap_gb.start()
    half_tile(mine)
    in_rmom.wait()
    swap_gr.wait()
    swap_gb.wait()
    value, moment = step(vrow[...], vrmom[...], gro[mine] + gin[...])
    vrow[...] = value
    vrmom[...] = moment
    rsend[...] = value.astype(BF16)
    value, moment = step(rb0[mine], rbm[...], gob[mine] + gib[...])
    rbsend[...] = value
    rbm[...] = moment
    go_rows = remote(rsend, rows1.at[mine], ssem.at[4], rsem.at[4], row=right)
    go_rows.start()
    go_rb = remote(rbsend, rb1.at[mine], ssem.at[5], rsem.at[5], row=right)
    go_rb.start()
    for j in range(EARLY, CHUNKS):
        push(j)

    def col_step():
        def body(s, carry):
            at = pl.ds(pl.multiple_of(s * 64, 64), 64)
            value, moment = step(vcol[at], vcmom[at], gc[at])
            vcol[at] = value
            vcmom[at] = moment
            col_low[at] = value.astype(BF16)
            return carry

        lax.fori_loop(0, cols // 64, body, 0)
        grad = jnp.sum(gcb[...], axis=0, keepdims=True)
        value, moment = step(cbias[...], cbm[...], grad)
        cbias[...] = value
        cbm[...] = moment

    in_cmom.wait()
    col_step()
    gc[...] = jnp.zeros_like(gc)
    gcb[...] = jnp.zeros_like(gcb)

    go_rows.wait()
    pass_rows = remote(rows1.at[mine], rows1.at[mine], ssem.at[6], rsem.at[6], col=other)
    pass_rows.start()
    go_rb.wait()
    pass_rb = remote(rb1.at[mine], rb1.at[mine], ssem.at[7], rsem.at[7], col=other)
    pass_rb.start()
    pass_rows.wait()
    pass_rb.wait()

    swaps = [
        remote(xs.at[j, other], xr.at[j], xsem.at[j], ysem.at[j], col=other)
        for j in range(CHUNKS)
    ]
    backs = [
        remote(bs.at[j], br.at[j], bsem.at[j], dsem.at[j], row=left)
        for j in range(CHUNKS)
    ]

    def give_back(j):
        swaps[j].wait()
        bs[j] = (xs[j, mine] + xr[j]).astype(BF16)
        backs[j].start()

    rbcol = [to_column(rb1[s]) for s in (0, 1)]
    for j in range(CHUNKS):
        send_counts[j].wait()
        at = slice(j * part, (j + 1) * part)

        def load(o):
            return rcv[j, pl.ds(o, SUB)].astype(F32)

        def store_sum(total):
            for s in (0, 1):
                bacc[s, at] = total[s * part:(s + 1) * part]

        rows = jnp.concatenate([rows1[0, at], rows1[1, at]], axis=0)
        bias = jnp.concatenate([rbcol[0][at], rbcol[1][at]], axis=0)
        grad = tile(rows, bias, load, store_sum)
        for s in (0, 1):
            xs[j, s] = grad[s * part:(s + 1) * part]
        swaps[j].start()
        if j > 0:
            give_back(j - 1)

    for s in (0, 1):
        xsb[s] = to_line(bacc[s])
    swap_b = remote(xsb.at[other], xrb, ssem.at[8], rsem.at[8], col=other)
    swap_b.start()
    give_back(CHUNKS - 1)
    swap_b.wait()
    bsb[...] = xsb[mine] + xrb[...]
    back_b = remote(bsb, brb, ssem.at[9], rsem.at[9], row=left)
    back_b.start()

    col_step()
    out_col = pltpu.make_async_copy(vcol, col_out, osem.at[0])
    out_col.start()
    col_bias_out[...] = cbias[...]

    for j in range(CHUNKS):
        backs[j].wait()
        at = slice(j * part, (j + 1) * part)
        value, moment = step(vrow[at], vrmom[at], br[j].astype(F32))
        vrow[at] = value
    out_row = pltpu.make_async_copy(vrow, row_out, osem.at[1])
    out_row.start()
    back_b.wait()
    value, moment = step(rbsend[...], rbm[...], brb[...])
    row_bias_out[...] = value
    out_col.wait()
    out_row.wait()


def per_device(
    ring,
    counts,
    row_factors,
    row_moments,
    row_bias,
    row_bias_moments,
    col_factors,
    col_moments,
    col_bias,
    col_bias_moments,
):
    rounds, height, cols = counts.shape
    half, rank = row_factors.shape
    part = half // CHUNKS
    hbm = pl.BlockSpec(memory_space=pl.ANY)
    vmem = pl.BlockSpec(memory_space=pltpu.VMEM)
    dma = pltpu.SemaphoreType.DMA
    scratch = [
        pltpu.VMEM((2, half, cols), jnp.int32),
        pltpu.VMEM((CHUNKS, 2, part, cols), jnp.int32),
        pltpu.VMEM((half, rank), F32),
        pltpu.VMEM((half, rank), F32),
        pltpu.VMEM((cols, rank), F32),
        pltpu.VMEM((cols, rank), F32),
        pltpu.VMEM((cols, rank), BF16),
        pltpu.VMEM((2, half, rank), BF16),
        pltpu.VMEM((2, 1, half), F32),
        pltpu.VMEM((2, half, rank), BF16),
        pltpu.VMEM((2, 1, half), F32),
        pltpu.VMEM((half, rank), BF16),
        pltpu.VMEM((1, half), F32),
        pltpu.VMEM((CHUNKS, 2 * part, cols), BF16),
        pltpu.VMEM((CHUNKS, 2 * part, cols), BF16),
        pltpu.VMEM((half, cols), F32),
        pltpu.VMEM((half, cols), BF16),
        pltpu.VMEM((half, LANES), F32),
        pltpu.VMEM((2, half, LANES), F32),
        pltpu.VMEM((2, half, rank), F32),
        pltpu.VMEM((half, rank), F32),
        pltpu.VMEM((2, 1, half), F32),
        pltpu.VMEM((1, half), F32),
        pltpu.VMEM((cols, rank), F32),
        pltpu.VMEM((8, cols), F32),
        pltpu.VMEM((1, half), F32),
        pltpu.VMEM((1, cols), F32),
        pltpu.VMEM((1, cols), F32),
        pltpu.VMEM((CHUNKS, 2, part, rank), F32),
        pltpu.VMEM((CHUNKS, part, rank), F32),
        pltpu.VMEM((CHUNKS, part, rank), BF16),
        pltpu.VMEM((CHUNKS, part, rank), BF16),
        pltpu.VMEM((2, 1, half), F32),
        pltpu.VMEM((1, half), F32),
        pltpu.VMEM((1, half), F32),
        pltpu.VMEM((1, half), F32),
        dma((5 + CHUNKS,)),
        dma((2,)),
        dma((10,)),
        dma((10,)),
        dma((CHUNKS,)),
        dma((CHUNKS,)),
        dma((CHUNKS,)),
        dma((CHUNKS,)),
        dma((CHUNKS,)),
        dma((CHUNKS,)),
    ]
    row_new, row_level, col_new, col_level = pl.pallas_call(
        functools.partial(kernel, ring),
        out_shape=(
            jax.ShapeDtypeStruct((half, rank), F32),
            jax.ShapeDtypeStruct((1, half), F32),
            jax.ShapeDtypeStruct((cols, rank), F32),
            jax.ShapeDtypeStruct((1, cols), F32),
        ),
        in_specs=[hbm, hbm, hbm, vmem, vmem, hbm, hbm, vmem, vmem],
        out_specs=(hbm, vmem, hbm, vmem),
        scratch_shapes=scratch,
        compiler_params=pltpu.CompilerParams(
            collective_id=0, has_side_effects=True, vmem_limit_bytes=48 * 1024 * 1024
        ),
    )(
        counts.reshape(rounds, 2, half, cols),
        row_factors,
        row_moments,
        row_bias.reshape(1, half),
        row_bias_moments.reshape(1, half),
        col_factors,
        col_moments,
        col_bias.reshape(1, cols),
        col_bias_moments.reshape(1, cols),
    )
    return row_new, row_level.reshape(half), col_new, col_level.reshape(cols)


def solution(mesh):
    in_specs = (
        P(None, ("groups", "row"), "col"),
        P(("groups", "row", "col"), None),
        P(("groups", "row", "col"), None),
        P(("groups", "row", "col")),
        P(("groups", "row", "col")),
        P(("groups", "row", "col"), None),
        P(("groups", "row", "col"), None),
        P(("groups", "row", "col")),
        P(("groups", "row", "col")),
    )
    out_specs = (
        P(("groups", "row", "col"), None),
        P(("groups", "row", "col")),
        P(("groups", "row", "col"), None),
        P(("groups", "row", "col")),
    )
    return jax.shard_map(
        functools.partial(per_device, mesh.shape["row"]),
        mesh=mesh, in_specs=in_specs, out_specs=out_specs, check_vma=False,
    )
```

time: 195 us -> 57 us (0.29)
  waiting for transfers between devices: 122 us -> 0 us
  Pallas kernels: 0 us -> 46.3 us
  matrix products: 21.5 us -> 0 us
  between operations: 14.8 us -> 0.66 us
  blocking collectives: 13.2 us -> 0 us
  starting transfers between devices: 13.1 us -> 0 us
  other arithmetic: 5.27 us -> 0 us
  local copies, waits for them, and re-layouts: 4.54 us -> 9.67 us
    ppermute x6 -> x0, waiting for transfers between devices: 122 us -> none  [from_behind(): return lax.ppermute(value, axis, pairs)]
    pallas_call x0 -> x1, Pallas kernels: none -> 46.3 us  [per_device(): pl.pallas_call(functools.partial(kernel, ring), out_shape=(jax.ShapeDtype...]
    dot_general x6 -> x0, matrix products: 21.5 us -> none  [the longest x2 9.43 us: tile_grads(): lax.dot_general(residue_low, gathered, (((0,), (0,)), ((), ())), preferre...]
    ppermute x6 -> x0, starting transfers between devices: 13 us -> none  [from_behind(): return lax.ppermute(value, axis, pairs)]
    all_gather x4 -> x0, blocking collectives: 8.27 us -> none  [the longest x2 4.36 us: per_device(): lax.all_gather(row_value.astype(jnp.bfloat16), 'col', axis=0, tiled=True)]
    unnamed x27 -> x18, local copies, waits for them, and re-layouts: 4.54 us -> 9.67 us
    unnamed x2 -> x0, blocking collectives: 4.94 us -> none
    sub x5 -> x0, other arithmetic: 2.98 us -> none  [adagrad(): return (current - LEARN_RATE * gradient / jnp.sqrt(moment), moment)]
  transfers between devices with their start and end apart: 8 -> 0, of which waited for: 3 -> 0; matrix products, arithmetic and copies ran while one was open for 10% -> 0% of each run, Pallas kernels for 0% -> 0%
where the time goes in v1:
time: 57 us; the launch traced here: 56.7 us
  Pallas kernels  46.3 us (81%)
  local copies, waits for them, and re-layouts  9.67 us (17%)
  between operations  0.66 us (1%)
    pallas_call x1, Pallas kernels, per_device(): pl.pallas_call(functools.partial(kernel, ring), out_shape=(jax.ShapeDtype...  46.3 us
    unnamed x18, local copies, waits for them, and re-layouts  9.67 us

profile of v1, /device:TPU:0, one launch (start us, length us, event | category | flops | bytes accessed | tf_op | source)
XLA Modules:
  0.0 56.7 jit_solution(7222125612492262470)
XLA Ops:
  0.6 0.0 copy-start
  0.6 1.6 %copy-done = f32[1024,512]{1,0:T(8,128)S(1)} copy-done((f32[1024,512]{1,0:T(8,128)S(1)}, f32[1024,512]{1,0:T(8,128)}, u32[]{:S(2)}) %copy-start) | copy-done | bytes 2097176
  2.2 0.0 copy-start.1
  2.2 1.0 %copy-done.1 = f32[256,512]{1,0:T(8,128)S(1)} copy-done((f32[256,512]{1,0:T(8,128)S(1)}, f32[256,512]{1,0:T(8,128)}, u32[]{:S(2)}) %copy-start.1) | copy-done | bytes 524312
  3.3 0.0 copy-start.2
  3.3 1.0 %copy-done.2 = f32[256,512]{1,0:T(8,128)S(1)} copy-done((f32[256,512]{1,0:T(8,128)S(1)}, f32[256,512]{1,0:T(8,128)}, u32[]{:S(2)}) %copy-start.2) | copy-done | bytes 524312
  4.3 0.0 copy-start.3
  4.3 0.7 %copy-done.3 = f32[1024]{0:T(1024)S(1)} copy-done((f32[1024]{0:T(1024)S(1)}, f32[1024]{0:T(1024)}, u32[]{:S(2)}) %copy-start.3) | copy-done | bytes 4120
  5.0 0.0 copy-start.4
  5.0 0.7 %copy-done.4 = f32[1024]{0:T(1024)S(1)} copy-done((f32[1024]{0:T(1024)S(1)}, f32[1024]{0:T(1024)}, u32[]{:S(2)}) %copy-start.4) | copy-done | bytes 4120
  5.7 0.0 copy-start.5
  5.7 0.7 %copy-done.5 = f32[256]{0:T(256)S(1)} copy-done((f32[256]{0:T(256)S(1)}, f32[256]{0:T(256)}, u32[]{:S(2)}) %copy-start.5) | copy-done | bytes 1048
  6.4 0.0 copy-start.6
  6.4 0.7 %copy-done.6 = f32[256]{0:T(256)S(1)} copy-done((f32[256]{0:T(256)S(1)}, f32[256]{0:T(256)}, u32[]{:S(2)}) %copy-start.6) | copy-done | bytes 1048
  7.0 46.3 %shard_map.120 = (f32[256,512]{1,0:T(8,128)S(1)}, f32[1,256]{1,0:T(1,128)S(1)}, f32[1024,512]{1,0:T(8,128)S(1)}, f32[1,1024]{1,0:T(1,128)S(1)}) custom-call(s32[2,2,256,1024]{3,2,1,0:T(8,128)} %bitcast.13, f32[256,512]{1,0:T(8,128)S(1)} %copy-done.1, f32[256,512]{1,0:T(8,128)S(1)} %copy-done.2, f32[1,256]{1,0:T(1,128)S(1)} %bitcast.10, ...), custom_call_target="tpu_custom_call" | custom-call | tf_op jit(solution)/shard_map/pallas_call | solution.py:345
  53.4 0.8 %copy.17 = f32[256,512]{1,0:T(8,128)} copy(f32[256,512]{1,0:T(8,128)S(1)} %get-tuple-element.16) | data formatting | bytes 1048576
  54.2 0.6 copy.18
  54.8 1.3 %copy.19 = f32[1024,512]{1,0:T(8,128)} copy(f32[1024,512]{1,0:T(8,128)S(1)} %get-tuple-element.18) | data formatting | bytes 4194304
  56.1 0.6 %copy.20 = f32[1024]{0:T(1024)} copy(f32[1024]{0:T(1024)S(1)} %bitcast.9) | data formatting | bytes 8192
Async XLA Ops:
  0.6 1.6 %copy-start = (f32[1024,512]{1,0:T(8,128)S(1)}, f32[1024,512]{1,0:T(8,128)}, u32[]{:S(2)}) copy-start(f32[1024,512]{1,0:T(8,128)} %col_factors.1) | copy-start | bytes 6291460
  2.2 1.0 %copy-start.1 = (f32[256,512]{1,0:T(8,128)S(1)}, f32[256,512]{1,0:T(8,128)}, u32[]{:S(2)}) copy-start(f32[256,512]{1,0:T(8,128)} %row_factors.1) | copy-start | bytes 1572868
  3.3 1.0 %copy-start.2 = (f32[256,512]{1,0:T(8,128)S(1)}, f32[256,512]{1,0:T(8,128)}, u32[]{:S(2)}) copy-start(f32[256,512]{1,0:T(8,128)} %row_moments.1) | copy-start | bytes 1572868
  4.3 0.7 %copy-start.3 = (f32[1024]{0:T(1024)S(1)}, f32[1024]{0:T(1024)}, u32[]{:S(2)}) copy-start(f32[1024]{0:T(1024)} %param.16) | copy-start | bytes 12292
  5.0 0.7 %copy-start.4 = (f32[1024]{0:T(1024)S(1)}, f32[1024]{0:T(1024)}, u32[]{:S(2)}) copy-start(f32[1024]{0:T(1024)} %param.17) | copy-start | bytes 12292
  5.7 0.7 %copy-start.5 = (f32[256]{0:T(256)S(1)}, f32[256]{0:T(256)}, u32[]{:S(2)}) copy-start(f32[256]{0:T(256)} %param.12) | copy-start | bytes 3076
  6.4 0.7 %copy-start.6 = (f32[256]{0:T(256)S(1)}, f32[256]{0:T(256)}, u32[]{:S(2)}) copy-start(f32[256]{0:T(256)} %param.13) | copy-start | bytes 3076

commit v2 on v1

--- a/solution.py
+++ b/solution.py
@@ -13,8 +13,10 @@
 COUNT_SCALE = 100.0
 WEIGHT_POWER = 0.75
 CHUNKS = 4
-EARLY = 2
+EARLY = 3
 SUB = 16
+UNROLL = 4
+BEFORE = 2
 LANES = 128
 MESH = pl.DeviceIdType.MESH
 F32 = jnp.float32
@@ -42,9 +44,9 @@
     c0, c1, vrow, vrmom, vcol, vcmom, col_low,
     rows0, rb0, rows1, rb1, rsend, rbsend, snd, rcv,
     pred, res, rbc, bacc, gro, gin, gob, gib, gc, gcb,
-    rbm, cbias, cbm,
+    rbm, cbias, cbm, wgt, lgs,
     xs, xr, bs, br, xsb, xrb, bsb, brb,
-    lsem, osem, ssem, rsem, csem, ksem, xsem, ysem,
+    lsem, ssem, rsem, csem, ksem, xsem, ysem,
     bsem, dsem,
 ):
     me = lax.axis_index("row")
@@ -68,6 +70,7 @@
         )
 
     in_row = local(row_factors, vrow, 0)
+    in_rb = local(row_bias, rb0.at[mine], 5 + CHUNKS)
     in_c1 = [
         local(counts.at[1, :, pl.ds(j * part, part), :], c1.at[j], 1 + j)
         for j in range(CHUNKS)
@@ -77,6 +80,12 @@
     in_rmom = local(row_moments, vrmom, 3 + CHUNKS)
     in_cmom = local(col_moments, vcmom, 4 + CHUNKS)
 
+    in_small = [
+        local(row_bias_mom, rbm, 6 + CHUNKS),
+        local(col_bias, cbias, 7 + CHUNKS),
+        local(col_bias_mom, cbm, 8 + CHUNKS),
+    ]
+
     barrier = pltpu.get_barrier_semaphore()
     pl.semaphore_signal(barrier, inc=1, device_id={"row": left}, device_id_type=MESH)
     pl.semaphore_signal(barrier, inc=1, device_id={"row": right}, device_id_type=MESH)
@@ -84,7 +93,7 @@
 
     in_row.wait()
     rows0[mine] = vrow[...].astype(BF16)
-    rb0[mine] = row_bias[...]
+    in_rb.wait()
     pl.semaphore_wait(barrier, 3)
     swap_rows = remote(rows0.at[mine], rows0.at[mine], ssem.at[0], rsem.at[0], col=other)
     swap_rows.start()
@@ -107,13 +116,16 @@
 
     in_col.wait()
     col_low[...] = vcol[...].astype(BF16)
-    cbias[...] = col_bias[...]
-    cbm[...] = col_bias_mom[...]
-    rbm[...] = row_bias_mom[...]
-    gc[...] = jnp.zeros_like(gc)
+    for cp in in_small:
+        cp.wait()
     gcb[...] = jnp.zeros_like(gcb)
 
-    def tile(rows, column_bias, load, store_sum):
+    def weigh(x):
+        logs = jnp.log(jnp.maximum(x, 1.0))
+        weight = jnp.exp(WEIGHT_POWER * (logs - math.log(COUNT_SCALE)))
+        return jnp.where(x >= 1.0, jnp.minimum(weight, 1.0), 0.0), logs
+
+    def residues(rows, column_bias, load, out):
         count = rows.shape[0]
         rbc[0:count] = column_bias
         pred[0:count] = lax.dot_general(
@@ -122,13 +134,10 @@
 
         def body(s, carry):
             o = pl.multiple_of(s * SUB, SUB)
-            x = load(o)
-            logs = jnp.log(jnp.maximum(x, 1.0))
-            weight = jnp.exp(WEIGHT_POWER * (logs - math.log(COUNT_SCALE)))
-            weight = jnp.where(x >= 1.0, jnp.minimum(weight, 1.0), 0.0)
+            weight, logs = load(o)
             bias = rbc[pl.ds(o, SUB)][:, 0:1]
             value = weight * (pred[pl.ds(o, SUB)] + bias + cbias[...] - logs)
-            res[pl.ds(o, SUB)] = value.astype(BF16)
+            out[pl.ds(o, SUB)] = value.astype(BF16)
             total = value[:, 0:LANES]
             for k in range(1, cols // LANES):
                 total = total + value[:, k * LANES:(k + 1) * LANES]
@@ -139,23 +148,32 @@
             gcb[...] += down
             return carry
 
-        lax.fori_loop(0, count // SUB, body, 0)
-        store_sum(rbc[0:count])
-        low = res[0:count]
-        grad_rows = jnp.dot(low, col_low[...], preferred_element_type=F32)
-        gc[...] += lax.dot_general(
+        lax.fori_loop(0, count // SUB, body, 0, unroll=UNROLL)
+
+    def col_grads(low, rows):
+        return lax.dot_general(
             low, rows, (((0,), (0,)), ((), ())), preferred_element_type=F32
         )
-        return grad_rows
 
     def half_tile(which):
         def load(o):
-            return c0[which, pl.ds(o, SUB)].astype(F32)
-
-        def store_sum(total):
-            gob[which] = to_line(total)
-
-        gro[which] = tile(rows0[which], to_column(rb0[which]), load, store_sum)
+            return weigh(c0[which, pl.ds(o, SUB)].astype(F32))
+
+        residues(rows0[which], to_column(rb0[which]), load, res.at[which])
+        gob[which] = to_line(rbc[...])
+        gro[which] = jnp.dot(res[which], col_low[...], preferred_element_type=F32)
+
+    def ready(j):
+        send_counts[j].wait()
+
+        def body(s, carry):
+            at = pl.ds(pl.multiple_of(s * SUB, SUB), SUB)
+            weight, logs = weigh(rcv[j, at].astype(F32))
+            wgt[j, at] = weight
+            lgs[j, at] = logs
+            return carry
+
+        lax.fori_loop(0, 2 * part // SUB, body, 0, unroll=UNROLL)
 
     swap_rows.wait()
     swap_rb.wait()
@@ -183,25 +201,32 @@
     for j in range(EARLY, CHUNKS):
         push(j)
 
-    def col_step():
+    def col_step(out):
         def body(s, carry):
             at = pl.ds(pl.multiple_of(s * 64, 64), 64)
             value, moment = step(vcol[at], vcmom[at], gc[at])
-            vcol[at] = value
-            vcmom[at] = moment
-            col_low[at] = value.astype(BF16)
+            out[at] = value
+            if out is vcol:
+                vcmom[at] = moment
+                col_low[at] = value.astype(BF16)
             return carry
 
         lax.fori_loop(0, cols // 64, body, 0)
         grad = jnp.sum(gcb[...], axis=0, keepdims=True)
         value, moment = step(cbias[...], cbm[...], grad)
-        cbias[...] = value
-        cbm[...] = moment
-
+        return value, moment
+
+    gc[...] = col_grads(
+        res[...].reshape(2 * half, cols), rows0[...].reshape(2 * half, rows0.shape[2])
+    )
     in_cmom.wait()
-    col_step()
-    gc[...] = jnp.zeros_like(gc)
+    value, moment = col_step(vcol)
+    cbias[...] = value
+    cbm[...] = moment
     gcb[...] = jnp.zeros_like(gcb)
+
+    for j in range(BEFORE):
+        ready(j)
 
     go_rows.wait()
     pass_rows = remote(rows1.at[mine], rows1.at[mine], ssem.at[6], rsem.at[6], col=other)
@@ -226,26 +251,32 @@
         bs[j] = (xs[j, mine] + xr[j]).astype(BF16)
         backs[j].start()
 
+    def add_col_grads(j, low, rows):
+        grad = col_grads(low[...], rows)
+        gc[...] = grad if j == 0 else gc[...] + grad
+
     rbcol = [to_column(rb1[s]) for s in (0, 1)]
     for j in range(CHUNKS):
-        send_counts[j].wait()
+        if j >= BEFORE:
+            ready(j)
         at = slice(j * part, (j + 1) * part)
 
         def load(o):
-            return rcv[j, pl.ds(o, SUB)].astype(F32)
-
-        def store_sum(total):
-            for s in (0, 1):
-                bacc[s, at] = total[s * part:(s + 1) * part]
+            return wgt[j, pl.ds(o, SUB)], lgs[j, pl.ds(o, SUB)]
 
         rows = jnp.concatenate([rows1[0, at], rows1[1, at]], axis=0)
         bias = jnp.concatenate([rbcol[0][at], rbcol[1][at]], axis=0)
-        grad = tile(rows, bias, load, store_sum)
+        low = res.at[j % 2, 0:2 * part]
+        residues(rows, bias, load, low)
+        grad = jnp.dot(low[...], col_low[...], preferred_element_type=F32)
         for s in (0, 1):
             xs[j, s] = grad[s * part:(s + 1) * part]
+            bacc[s, at] = rbc[s * part:(s + 1) * part]
         swaps[j].start()
         if j > 0:
             give_back(j - 1)
+        if j < CHUNKS - 1:
+            add_col_grads(j, low, rows)
 
     for s in (0, 1):
         xsb[s] = to_line(bacc[s])
@@ -257,23 +288,30 @@
     back_b = remote(bsb, brb, ssem.at[9], rsem.at[9], row=left)
     back_b.start()
 
-    col_step()
-    out_col = pltpu.make_async_copy(vcol, col_out, osem.at[0])
-    out_col.start()
-    col_bias_out[...] = cbias[...]
+    add_col_grads(CHUNKS - 1, low, rows)
+    value, moment = col_step(col_out)
+    col_bias_out[...] = value
 
     for j in range(CHUNKS):
         backs[j].wait()
         at = slice(j * part, (j + 1) * part)
         value, moment = step(vrow[at], vrmom[at], br[j].astype(F32))
-        vrow[at] = value
-    out_row = pltpu.make_async_copy(vrow, row_out, osem.at[1])
-    out_row.start()
+        row_out[at] = value
     back_b.wait()
     value, moment = step(rbsend[...], rbm[...], brb[...])
     row_bias_out[...] = value
-    out_col.wait()
-    out_row.wait()
+
+
+def leave(*refs):
+    sem = refs[-1]
+    count = len(refs) // 2
+    copies = [
+        pltpu.make_async_copy(refs[k], refs[count + k], sem.at[k]) for k in range(count)
+    ]
+    for cp in copies:
+        cp.start()
+    for cp in copies:
+        cp.wait()
 
 
 def per_device(
@@ -291,7 +329,7 @@
     rounds, height, cols = counts.shape
     half, rank = row_factors.shape
     part = half // CHUNKS
-    hbm = pl.BlockSpec(memory_space=pl.ANY)
+    hbm = pl.BlockSpec(memory_space=pltpu.HBM)
     vmem = pl.BlockSpec(memory_space=pltpu.VMEM)
     dma = pltpu.SemaphoreType.DMA
     scratch = [
@@ -311,7 +349,7 @@
         pltpu.VMEM((CHUNKS, 2 * part, cols), BF16),
         pltpu.VMEM((CHUNKS, 2 * part, cols), BF16),
         pltpu.VMEM((half, cols), F32),
-        pltpu.VMEM((half, cols), BF16),
+        pltpu.VMEM((2, half, cols), BF16),
         pltpu.VMEM((half, LANES), F32),
         pltpu.VMEM((2, half, LANES), F32),
         pltpu.VMEM((2, half, rank), F32),
@@ -323,6 +361,8 @@
         pltpu.VMEM((1, half), F32),
         pltpu.VMEM((1, cols), F32),
         pltpu.VMEM((1, cols), F32),
+        pltpu.VMEM((CHUNKS, 2 * part, cols), F32),
+        pltpu.VMEM((CHUNKS, 2 * part, cols), F32),
         pltpu.VMEM((CHUNKS, 2, part, rank), F32),
         pltpu.VMEM((CHUNKS, part, rank), F32),
         pltpu.VMEM((CHUNKS, part, rank), BF16),
@@ -331,8 +371,7 @@
         pltpu.VMEM((1, half), F32),
         pltpu.VMEM((1, half), F32),
         pltpu.VMEM((1, half), F32),
-        dma((5 + CHUNKS,)),
-        dma((2,)),
+        dma((9 + CHUNKS,)),
         dma((10,)),
         dma((10,)),
         dma((CHUNKS,)),
@@ -342,19 +381,15 @@
         dma((CHUNKS,)),
         dma((CHUNKS,)),
     ]
-    row_new, row_level, col_new, col_level = pl.pallas_call(
+    shapes = ((half, rank), (1, half), (cols, rank), (1, cols))
+    found = pl.pallas_call(
         functools.partial(kernel, ring),
-        out_shape=(
-            jax.ShapeDtypeStruct((half, rank), F32),
-            jax.ShapeDtypeStruct((1, half), F32),
-            jax.ShapeDtypeStruct((cols, rank), F32),
-            jax.ShapeDtypeStruct((1, cols), F32),
-        ),
-        in_specs=[hbm, hbm, hbm, vmem, vmem, hbm, hbm, vmem, vmem],
-        out_specs=(hbm, vmem, hbm, vmem),
+        out_shape=[pltpu.VMEM(shape, F32) for shape in shapes],
+        in_specs=[hbm] * 9,
+        out_specs=[vmem] * 4,
         scratch_shapes=scratch,
         compiler_params=pltpu.CompilerParams(
-            collective_id=0, has_side_effects=True, vmem_limit_bytes=48 * 1024 * 1024
+            collective_id=0, has_side_effects=True, vmem_limit_bytes=56 * 1024 * 1024
         ),
     )(
         counts.reshape(rounds, 2, half, cols),
@@ -367,6 +402,14 @@
         col_bias.reshape(1, cols),
         col_bias_moments.reshape(1, cols),
     )
+    row_new, row_level, col_new, col_level = pl.pallas_call(
+        leave,
+        out_shape=[jax.ShapeDtypeStruct(shape, F32) for shape in shapes],
+        in_specs=[vmem] * 4,
+        out_specs=[hbm] * 4,
+        scratch_shapes=[dma((4,))],
+        compiler_params=pltpu.CompilerParams(vmem_limit_bytes=2 * 1024 * 1024),
+    )(*found)
     return row_new, row_level.reshape(half), col_new, col_level.reshape(cols)
 
 

time: 57 us -> 46.2 us (0.81)
  local copies, waits for them, and re-layouts: 9.67 us -> 0 us
  Pallas kernels: 46.3 us -> 45.4 us
    unnamed x18 -> x0, local copies, waits for them, and re-layouts: 9.67 us -> none
    pallas_call x1 -> x2, Pallas kernels: 46.3 us -> 45.4 us  [the longest x1 43.9 us: per_device(): pl.pallas_call(functools.partial(kernel, ring), out_shape=[pltpu.VMEM(sha...]
where the time goes in v2:
time: 46.2 us; the launch traced here: 46.1 us
  Pallas kernels  45.4 us (98%)
  between operations  0.64 us (1%)
    pallas_call x1, Pallas kernels, per_device(): pl.pallas_call(functools.partial(kernel, ring), out_shape=[pltpu.VMEM(sha...  43.9 us
    pallas_call x1, Pallas kernels, per_device(): pl.pallas_call(leave, out_shape=[jax.ShapeDtypeStruct(shape, F32) for sha...  1.54 us

profile of v2, /device:TPU:0, one launch (start us, length us, event | category | flops | bytes accessed | tf_op | source)
XLA Modules:
  0.0 46.1 jit_solution(4434840109603970623)
XLA Ops:
  0.6 43.9 %shard_map.120 = (f32[256,512]{1,0:T(8,128)S(1)}, f32[1,256]{1,0:T(1,128)S(1)}, f32[1024,512]{1,0:T(8,128)S(1)}, f32[1,1024]{1,0:T(1,128)S(1)}) custom-call(s32[2,2,256,1024]{3,2,1,0:T(8,128)} %bitcast.7, f32[256,512]{1,0:T(8,128)} %row_factors.1, f32[256,512]{1,0:T(8,128)} %row_moments.1, f32[1,256]{1,0:T(1,128)} %bitcast.10, f32[1,256]{1,0:T(1,128)} %bitcast.11, ...), custom_call_target="tpu_custom_call" | custom-call | tf_op jit(solution)/shard_map/pallas_call | solution.py:385
  44.6 1.5 %shard_map.121 = (f32[256,512]{1,0:T(8,128)}, f32[1,256]{1,0:T(1,128)}, f32[1024,512]{1,0:T(8,128)}, f32[1,1024]{1,0:T(1,128)}) custom-call(f32[256,512]{1,0:T(8,128)S(1)} %get-tuple-element.12.refs_0_, f32[1,256]{1,0:T(1,128)S(1)} %get-tuple-element.13.refs_1_, f32[1024,512]{1,0:T(8,128)S(1)} %get-tuple-element.14.refs_2_, ...), custom_call_target="tpu_custom_call" | custom-call | tf_op jit(solution)/shard_map/pallas_call | solution.py:405

commit v3 on v2

--- a/solution.py
+++ b/solution.py
@@ -16,7 +16,7 @@
 EARLY = 3
 SUB = 16
 UNROLL = 4
-BEFORE = 2
+BEFORE = 3
 LANES = 128
 MESH = pl.DeviceIdType.MESH
 F32 = jnp.float32

time: 46.2 us -> 47.3 us (1.024)
  Pallas kernels: 45.4 us -> 46.5 us
    pallas_call x1, Pallas kernels: 43.9 us -> 45 us  [per_device(): pl.pallas_call(functools.partial(kernel, ring), out_shape=[pltpu.VMEM(sha...]
where the time goes in v3:
time: 47.3 us; the launch traced here: 47.2 us
  Pallas kernels  46.5 us (98%)
  between operations  0.64 us (1%)
    pallas_call x1, Pallas kernels, per_device(): pl.pallas_call(functools.partial(kernel, ring), out_shape=[pltpu.VMEM(sha...  45 us
    pallas_call x1, Pallas kernels, per_device(): pl.pallas_call(leave, out_shape=[jax.ShapeDtypeStruct(shape, F32) for sha...  1.54 us

profile of v3, /device:TPU:0, one launch (start us, length us, event | category | flops | bytes accessed | tf_op | source)
XLA Modules:
  0.0 47.2 jit_solution(8681677059707646970)
XLA Ops:
  0.6 45.0 %shard_map.120 = (f32[256,512]{1,0:T(8,128)S(1)}, f32[1,256]{1,0:T(1,128)S(1)}, f32[1024,512]{1,0:T(8,128)S(1)}, f32[1,1024]{1,0:T(1,128)S(1)}) custom-call(s32[2,2,256,1024]{3,2,1,0:T(8,128)} %bitcast.7, f32[256,512]{1,0:T(8,128)} %row_factors.1, f32[256,512]{1,0:T(8,128)} %row_moments.1, f32[1,256]{1,0:T(1,128)} %bitcast.10, f32[1,256]{1,0:T(1,128)} %bitcast.11, ...), custom_call_target="tpu_custom_call" | custom-call | tf_op jit(solution)/shard_map/pallas_call | solution.py:385
  45.6 1.5 %shard_map.121 = (f32[256,512]{1,0:T(8,128)}, f32[1,256]{1,0:T(1,128)}, f32[1024,512]{1,0:T(8,128)}, f32[1,1024]{1,0:T(1,128)}) custom-call(f32[256,512]{1,0:T(8,128)S(1)} %get-tuple-element.12.refs_0_, f32[1,256]{1,0:T(1,128)S(1)} %get-tuple-element.13.refs_1_, f32[1024,512]{1,0:T(8,128)S(1)} %get-tuple-element.14.refs_2_, ...), custom_call_target="tpu_custom_call" | custom-call | tf_op jit(solution)/shard_map/pallas_call | solution.py:405
